TPU v7x, 256 devices: a whole 4x4x8 slice. The times are simulated.
256 devices in a mesh: dp: 4 (over y_lo, core), expert: 8 (over z), tensor: 8 (over x, y_hi).
Axes of the slice: x: 4, y: 4 (y_hi: 2, y_lo: 2; y = y_hi * 2 + y_lo), z: 8, core: 2. Of those that a mesh axis runs over, the one named last changes fastest.
Arguments:
- grad_out: bfloat16 [32768, 2048], P(('dp', 'expert', 'tensor')), may hold values from -6 to 6
- expert_ids: int32 [32768, 2], P(('dp', 'expert', 'tensor')), may hold values from 0 to 63, all different within a row; in each aligned block of 128 rows (0 to 127, 128 to 255, ...) at most 5 rows name the same one
- gate_weights: float32 [32768, 2], P(('dp', 'expert', 'tensor')), may hold values from 0.05 to 0.6
- overflow: int32 [32768, 2], P(('dp', 'expert', 'tensor')), may hold values 0 or 1
- saved_gate: bfloat16 [64, 4, 64, 5, 1408], P(('expert', 'tensor'), None, None, None, 'dp'), may hold values from -6 to 6
- saved_up: bfloat16 [64, 4, 64, 5, 1408], P(('expert', 'tensor'), None, None, None, 'dp'), may hold values from -6 to 6
- w_gate: bfloat16 [64, 2048, 1408], P(('expert', 'tensor'), None, 'dp'), may hold values from -0.125 to 0.125
- w_up: bfloat16 [64, 2048, 1408], P(('expert', 'tensor'), None, 'dp'), may hold values from -0.125 to 0.125
- w_down: bfloat16 [64, 1408, 2048], P(('expert', 'tensor'), 'dp'), may hold values from -0.15625 to 0.15625
- shared_gate_act: bfloat16 [32768, 1408], P(('dp', 'expert'), 'tensor'), may hold values from -6 to 6
- shared_up_act: bfloat16 [32768, 1408], P(('dp', 'expert'), 'tensor'), may hold values from -6 to 6
- ws_gate: bfloat16 [2048, 1408], P(None, 'tensor'), may hold values from -0.125 to 0.125
- ws_up: bfloat16 [2048, 1408], P(None, 'tensor'), may hold values from -0.125 to 0.125
- ws_down: bfloat16 [1408, 2048], P('tensor'), may hold values from -0.15625 to 0.15625
- w_out: bfloat16 [2048, 2048], P('tensor'), may hold values from -0.125 to 0.125
Outputs:
- grad_hidden: bfloat16 [32768, 2048], P(('dp', 'expert', 'tensor'))
- grad_context: bfloat16 [32768, 2048], P(('dp', 'expert'), 'tensor')
Inputs may be any that keep to these rules, and one draw needn't show every extreme that they name: `expert_ids`: each row names 2 different experts; within the rows of one device (aligned blocks of 128 rows) no expert is named by more than 5 rows, a bound that some block reaches.
All inputs are finite; a program needn't handle non-finite values. No bound on the sum of `overflow` on one device may be relied on, other than what follows from the above.
Results may differ from a plain program's by a relative error of at most 0.015.
Values may be sent and summed in bfloat16 or wider, within the bound.
A program may use at most 128 MiB of HBM per device.

v0:
```python
import jax
import jax.numpy as jnp
from jax import lax
from jax.sharding import PartitionSpec as P


def rank_in_block(pair_experts, expert_total):
    onehot = (pair_experts[:, None] == jnp.arange(expert_total, dtype=jnp.int32)[None, :]).astype(
        jnp.int32
    )
    earlier = jnp.cumsum(onehot, axis=0) - onehot
    return jnp.sum(earlier * onehot, axis=1)


def fill_slots(pair_grads, pair_experts, expert_total, capacity):
    pair_count, model_width = pair_grads.shape
    destination = pair_experts * capacity + rank_in_block(pair_experts, expert_total)
    source = jnp.full((expert_total * capacity,), pair_count, jnp.int32)
    source = source.at[destination].set(jnp.arange(pair_count, dtype=jnp.int32))
    padded = jnp.concatenate([pair_grads, jnp.zeros((1, model_width), pair_grads.dtype)], axis=0)
    return (padded[source].reshape(expert_total, capacity, model_width), destination)


def weighted_pairs(grads, weights):
    scaled = grads.astype(jnp.float32)[:, None, :] * weights.astype(jnp.float32)[:, :, None]
    return scaled.astype(jnp.bfloat16).reshape(-1, grads.shape[1])


def swiglu_backward(hidden_activation, gate_act, up_act):
    gate_value = gate_act.astype(jnp.float32)
    sigmoid_value = jax.nn.sigmoid(gate_value)
    gate_input_gradient = (
        hidden_activation
        * up_act.astype(jnp.float32)
        * sigmoid_value
        * (1.0 + gate_value * (1.0 - sigmoid_value))
    ).astype(jnp.bfloat16)
    up_input_gradient = (hidden_activation * gate_value * sigmoid_value).astype(jnp.bfloat16)
    return (gate_input_gradient, up_input_gradient)


def expert_terms(
    capacity_slot_rows,
    gate_act,
    up_act,
    gate_projection_weight,
    up_projection_weight,
    down_projection_weight,
):
    hidden_activation = jnp.einsum(
        "cyg,cog->cyo",
        capacity_slot_rows,
        down_projection_weight,
        preferred_element_type=jnp.float32,
    )
    gate_input_gradient, up_input_gradient = swiglu_backward(hidden_activation, gate_act, up_act)
    input_gradient_output = jnp.einsum(
        "etv,ebv->etb",
        gate_input_gradient,
        gate_projection_weight,
        preferred_element_type=jnp.float32,
    )
    input_gradient_output = input_gradient_output + jnp.einsum(
        "etv,ebv->etb", up_input_gradient, up_projection_weight, preferred_element_type=jnp.float32
    )
    return lax.optimization_barrier(input_gradient_output.astype(jnp.bfloat16))


def body(
    grad_out,
    expert_ids,
    gate_weights,
    overflow,
    saved_gate,
    saved_up,
    w_gate,
    w_up,
    w_down,
    shared_gate_act,
    shared_up_act,
    ws_gate,
    ws_up,
    ws_down,
    w_out,
):
    dp_count = lax.axis_size("dp")
    group_count = lax.axis_size(("expert", "tensor"))
    expert_local, unused_dp, unused_group, capacity, unit_part = saved_gate.shape
    expert_total = expert_local * group_count
    token_count, model_width = grad_out.shape
    top_count = expert_ids.shape[1]
    flag_values = overflow.astype(jnp.float32)
    routed_weight = (gate_weights * (1.0 - flag_values)).astype(jnp.bfloat16)
    shared_weight = 1.0 + jnp.sum(gate_weights * flag_values, axis=1)
    pair_grads = weighted_pairs(grad_out, routed_weight)
    filled, destination = fill_slots(pair_grads, expert_ids.reshape(-1), expert_total, capacity)
    arrived = lax.all_to_all(
        filled[:, None], ("expert", "tensor"), split_axis=0, concat_axis=1, tiled=True
    )
    everyone = lax.all_gather(arrived[:, None], "dp", axis=1, tiled=True)
    terms = expert_terms(
        everyone.reshape(expert_local, -1, model_width),
        saved_gate.reshape(expert_local, -1, unit_part),
        saved_up.reshape(expert_local, -1, unit_part),
        w_gate,
        w_up,
        w_down,
    )
    terms = terms.astype(jnp.float32).reshape(
        expert_local, dp_count, group_count, capacity, model_width
    )
    summed = lax.psum_scatter(
        terms.astype(jnp.bfloat16), "dp", scatter_dimension=1, tiled=True
    ).astype(jnp.float32)
    returned = lax.all_to_all(
        summed[:, 0].astype(jnp.bfloat16),
        ("expert", "tensor"),
        split_axis=1,
        concat_axis=0,
        tiled=True,
    ).astype(jnp.float32)
    picked = returned.reshape(expert_total * capacity, model_width)[destination]
    routed = jnp.sum(picked.reshape(token_count, top_count, model_width), axis=1)
    routed_total = routed.astype(jnp.bfloat16)
    shared_grad = (grad_out.astype(jnp.float32) * shared_weight[:, None]).astype(jnp.bfloat16)
    group_shared = lax.all_gather(shared_grad, "tensor", axis=0, tiled=True)
    shared_hidden = jnp.einsum(
        "td,fd->tf", group_shared, ws_down, preferred_element_type=jnp.float32
    )
    shared_gate_grad, shared_up_grad = swiglu_backward(
        shared_hidden, shared_gate_act, shared_up_act
    )
    partial_value = jnp.einsum(
        "tf,df->td", shared_gate_grad, ws_gate, preferred_element_type=jnp.float32
    )
    partial_value = partial_value + jnp.einsum(
        "tf,df->td", shared_up_grad, ws_up, preferred_element_type=jnp.float32
    )
    partial_value = lax.optimization_barrier(partial_value.astype(jnp.bfloat16)).astype(jnp.float32)
    shared_total = lax.psum(partial_value.astype(jnp.bfloat16), "tensor").astype(jnp.float32)
    group_grads, group_routed = (
        lax.all_gather(grad_out, "tensor", axis=0, tiled=True),
        lax.all_gather(routed_total, "tensor", axis=0, tiled=True),
    )
    grad_group = (
        group_grads.astype(jnp.float32) + shared_total + group_routed.astype(jnp.float32)
    ).astype(jnp.bfloat16)
    position = lax.axis_index("tensor") * token_count
    grad_hidden = lax.dynamic_slice_in_dim(grad_group, position, token_count, 0)
    grad_context = jnp.einsum(
        "td,hd->th", grad_group, w_out, preferred_element_type=jnp.float32
    ).astype(jnp.bfloat16)
    return (grad_hidden, grad_context)


def solution(mesh):
    in_specs = (
        P(("dp", "expert", "tensor"), None),
        P(("dp", "expert", "tensor"), None),
        P(("dp", "expert", "tensor"), None),
        P(("dp", "expert", "tensor"), None),
        P(("expert", "tensor"), None, None, None, "dp"),
        P(("expert", "tensor"), None, None, None, "dp"),
        P(("expert", "tensor"), None, "dp"),
        P(("expert", "tensor"), None, "dp"),
        P(("expert", "tensor"), "dp", None),
        P(("dp", "expert"), "tensor"),
        P(("dp", "expert"), "tensor"),
        P(None, "tensor"),
        P(None, "tensor"),
        P("tensor", None),
        P("tensor", None),
    )
    out_specs = (P(("dp", "expert", "tensor"), None), P(("dp", "expert"), "tensor"))
    return jax.shard_map(body, mesh=mesh, in_specs=in_specs, out_specs=out_specs, check_vma=False)
```

profile of v0, /device:TPU:1, one launch (start us, length us, event | category | flops | bytes accessed | tf_op | source)
XLA Modules:
  0.0 691.3 jit_solution(10206642360038884631)
XLA Ops:
  12.7 2.1 mul.107
  14.8 2.5 mul.108
  19.2 3.0 gather_fusion
  22.2 2.4 broadcast_in_dim_reshape.4
  24.6 63.7 %all_to_all.8 = bf16[64,1,5,2048]{3,2,1,0:T(8,128)(2,1)S(1)} all-to-all(bf16[64,1,5,2048]{3,2,1,0:T(8,128)(2,1)S(1)} %bitcast.47), channel_id=1, replica_groups=mesh['dp'=4,'expert'=8,'tensor'=8] {'expert','tensor'}, dimensions={0} | all-to-all | bytes 2621440 | tf_op jit(solution)/shard_map/all_to_all | solution.py:97
  91.5 2.3 copy.40
  93.7 3.6 reshape.159
  99.2 3.5 copy.38
  102.7 3.7 reshape.158
  106.4 2.8 copy.39
  109.2 38.2 %all-gather.12.cloned.1.call-done = bf16[256,1,5,2048]{3,0,2,1:T(8,128)(2,1)} async-done(((bf16[64,1,5,2048]{3,0,2,1:T(8,128)(2,1)}), bf16[256,1,5,2048]{3,0,2,1:T(8,128)(2,1)}) %all-gather.12.cloned.1.call-update) | async-done | bytes 5242896 | tf_op jit(solution)/shard_map/all_gather | solution.py:100
  147.4 8.9 %copy.37 = bf16[256,1,5,2048]{3,2,0,1:T(8,128)(2,1)} copy(bf16[256,1,5,2048]{3,0,2,1:T(8,128)(2,1)} %all-gather.12.cloned.1.call-done) | data formatting | bytes 10485760 | tf_op jit(solution)/shard_map/all_gather | solution.py:100
  156.3 10.1 %reshape.152 = bf16[1280,2048]{1,0:T(8,128)(2,1)} reshape(bf16[256,1,5,2048]{3,2,0,1:T(8,128)(2,1)} %copy.37) | data formatting | bytes 10485760 | tf_op jit(solution)/shard_map/reshape.6
  166.4 5.1 fusion.4
  171.6 3.3 fusion.2
  174.9 5.0 fusion
  179.9 9.8 %convert_element_type.145 = bf16[1,4,64,5,2048]{4,3,2,1,0:T(8,128)(2,1)} reshape(bf16[1,1280,2048]{2,1,0:T(8,128)(2,1)} %fusion) | data formatting | bytes 10485760 | tf_op jit(solution)/shard_map/convert_element_type | solution.py:113
  190.4 37.0 %all-gather.8.cloned.1.call-done = bf16[1024,2048]{1,0:T(8,128)(2,1)} async-done(((bf16[128,2048]{1,0:T(8,128)(2,1)}), bf16[1024,2048]{1,0:T(8,128)(2,1)}) %all-gather.8.cloned.1.call-update) | async-done | bytes 4194320 | tf_op jit(solution)/shard_map/all_gather | solution.py:126
  227.4 3.7 fusion.32
  232.6 3.3 add_convert_fusion.2
  235.9 74.4 %reduce-scatter.2.cloned.1.call-done = bf16[1,1,64,5,2048]{4,3,2,1,0:T(8,128)(2,1)} async-done(((bf16[1,4,64,5,2048]{4,3,2,1,0:T(8,128)(2,1)}), bf16[1,1,64,5,2048]{4,3,2,1,0:T(8,128)(2,1)}) %reduce-scatter.2.cloned.1.call-update) | async-done | bytes 1310736 | tf_op jit(solution)/shard_map/reduce_scatter | solution.py:112
  310.2 12.6 %all-to-all-start.1 = ((bf16[1,64,5,2048]{3,2,0,1:T(8,128)(2,1)}), bf16[1,64,5,2048]{3,2,0,1:T(8,128)(2,1)}, u32[]{:S(2)}, u32[]{:S(2)}) async-start(bf16[1,64,5,2048]{3,2,0,1:T(8,128)(2,1)} %bitcast.48), calls=%async_computation.2 | async-start | bytes 4194304 | tf_op jit(solution)/shard_map/all_to_all | solution.py:115
  322.9 49.1 %all-to-all-done.1 = bf16[1,64,5,2048]{3,2,0,1:T(8,128)(2,1)} async-done(((bf16[1,64,5,2048]{3,2,0,1:T(8,128)(2,1)}), bf16[1,64,5,2048]{3,2,0,1:T(8,128)(2,1)}, u32[]{:S(2)}, u32[]{:S(2)}) %all-to-all-start.1) | async-done | bytes 1310752 | tf_op jit(solution)/shard_map/all_to_all | solution.py:115
  372.0 2.5 reshape.160
  374.5 2.7 gather_fusion.1
  377.2 2.5 reshape.156
  379.7 3.8 reduce_sum.32
  383.5 18.9 %all-gather.6.cloned.1.call-done = bf16[1024,2048]{1,0:T(8,128)(2,1)} async-done(((bf16[128,2048]{1,0:T(8,128)(2,1)}), bf16[1024,2048]{1,0:T(8,128)(2,1)}) %all-gather.6.cloned.1.call-update) | async-done | bytes 4194320 | tf_op jit(solution)/shard_map/all_gather | solution.py:142
  402.4 190.3 %all-reduce.3.cloned.1.call-done = bf16[1024,2048]{1,0:T(8,128)(2,1)} async-done(((bf16[1024,2048]{1,0:T(8,128)(2,1)}), bf16[1024,2048]{1,0:T(8,128)(2,1)}) %all-reduce.3.cloned.1.call-update) | async-done | bytes 4194320 | tf_op jit(solution)/shard_map/psum | solution.py:140
  592.7 81.1 %all-gather.10.cloned.1.call-done = bf16[1024,2048]{1,0:T(8,128)(2,1)} async-done(((bf16[128,2048]{1,0:T(8,128)(2,1)}), bf16[1024,2048]{1,0:T(8,128)(2,1)}) %all-gather.10.cloned.1.call-update) | async-done | bytes 4194320 | tf_op jit(solution)/shard_map/all_gather | solution.py:143
  673.9 7.6 %add_convert_fusion.1 = bf16[1024,2048]{1,0:T(8,128)(2,1)S(1)} fusion(bf16[1024,2048]{1,0:T(8,128)(2,1)} %all-gather.10.cloned.1.call-done, bf16[1024,2048]{1,0:T(8,128)(2,1)} %all-reduce.3.cloned.1.call-done, bf16[1024,2048]{1,0:T(8,128)(2,1)} %all-gather.6.cloned.1.call-done), kind=kLoop, calls=%fused_computation.4 | loop fusion | flops 12582912 | bytes 16777216 | tf_op jit(solution)/shard_map/convert_element_type | solution.py:147
  682.3 2.1 convolution_convert_fusion
  (65 shorter events, 15.4 us)
Async XLA Ops:
  7.2 164.4 %copy-start = (bf16[1,2048,352]{1,2,0:T(8,128)(2,1)S(1)}, bf16[1,2048,352]{1,2,0:T(8,128)(2,1)}, u32[]{:S(2)}) copy-start(bf16[1,2048,352]{1,2,0:T(8,128)(2,1)} %param.21) | copy-start | bytes 4325380
  7.2 140.2 %all-gather.12.cloned.1.call-start = ((), (), s32[]{:S(2)}) async-start(), calls=%async_computation.8 | async-start | bytes 6553600 | tf_op jit(solution)/shard_map/all_gather | solution.py:100
  88.2 2.0 copy-start.3
  90.2 1.3 copy-start.6
  90.2 137.1 %all-gather.8.cloned.1.call-start = ((), (), s32[]{:S(2)}) async-start(), calls=%async_computation.4 | async-start | bytes 4718592 | tf_op jit(solution)/shard_map/all_gather | solution.py:126
  91.3 219.0 %reduce-scatter.2.cloned.1.call-start = ((), (), s32[]{:S(2)}) async-start(), calls=%async_computation.6 | async-start | bytes 10485760 | tf_op jit(solution)/shard_map/reduce_scatter | solution.py:112
  166.4 5.1 copy-start.2
  171.6 3.3 copy-start.5
  189.7 37.7 %copy-start.11 = (bf16[176,2048]{1,0:T(8,128)(2,1)S(1)}, bf16[176,2048]{1,0:T(8,128)(2,1)}, u32[]{:S(2)}) copy-start(bf16[176,2048]{1,0:T(8,128)(2,1)} %param.28) | copy-start | bytes 2162692
  189.7 212.7 %all-gather.6.cloned.1.call-start = ((), (), s32[]{:S(2)}) async-start(), calls=%async_computation.3 | async-start | bytes 4718592 | tf_op jit(solution)/shard_map/all_gather | solution.py:142
  190.3 40.8 %copy-start.4 = (bf16[1024,176]{0,1:T(8,128)(2,1)S(1)}, bf16[1024,176]{0,1:T(8,128)(2,1)}, u32[]{:S(2)}) copy-start(bf16[1024,176]{0,1:T(8,128)(2,1)} %param.24) | copy-start | bytes 1081348
  190.3 40.8 %copy-start.8 = (bf16[2048,176]{0,1:T(8,128)(2,1)S(1)}, bf16[2048,176]{0,1:T(8,128)(2,1)}, u32[]{:S(2)}) copy-start(bf16[2048,176]{0,1:T(8,128)(2,1)} %param.26) | copy-start | bytes 2162692
  190.3 40.8 %copy-start.9 = (bf16[1024,176]{0,1:T(8,128)(2,1)S(1)}, bf16[1024,176]{0,1:T(8,128)(2,1)}, u32[]{:S(2)}) copy-start(bf16[1024,176]{0,1:T(8,128)(2,1)} %param.25) | copy-start | bytes 1081348
  190.3 402.4 %all-reduce.3.cloned.1.call-start = ((), (), s32[]{:S(2)}) async-start(), calls=%async_computation.5 | async-start | bytes 8388608 | tf_op jit(solution)/shard_map/psum | solution.py:140
  231.1 1.4 copy-start.7
  310.2 61.7 %all-to-all-start.1 = ((bf16[1,64,5,2048]{3,2,0,1:T(8,128)(2,1)}), bf16[1,64,5,2048]{3,2,0,1:T(8,128)(2,1)}, u32[]{:S(2)}, u32[]{:S(2)}) async-start(bf16[1,64,5,2048]{3,2,0,1:T(8,128)(2,1)} %bitcast.48), calls=%async_computation.2 | async-start | bytes 4194304 | tf_op jit(solution)/shard_map/all_to_all | solution.py:115
  322.8 351.0 %all-gather.10.cloned.1.call-start = ((), (), s32[]{:S(2)}) async-start(), calls=%async_computation.7 | async-start | bytes 4718592 | tf_op jit(solution)/shard_map/all_gather | solution.py:143
  383.5 298.8 %copy-start.10 = (bf16[256,2048]{1,0:T(8,128)(2,1)S(1)}, bf16[256,2048]{1,0:T(8,128)(2,1)}, u32[]{:S(2)}) copy-start(bf16[256,2048]{1,0:T(8,128)(2,1)} %param.29) | copy-start | bytes 3145732
  682.3 2.1 copy-start.1
Sparse Core Ops, SparseCore 0:
  90.4 57.0 all-gather.11
  150.6 76.7 all-gather.7
  230.0 80.2 reduce-scatter.1
  312.7 89.6 all-gather.5
  404.9 187.7 all-reduce.2
  595.8 78.0 all-gather.9
where the time goes:
time: 693 us; the launch traced here: 691 us
  waiting for transfers between devices  490 us (71%)
  local copies, waits for them, and re-layouts  70.6 us (10%)
  blocking collectives  63.7 us (9%)
  matrix products  24 us (3%)
  other arithmetic  16.3 us (2%)
  between operations  14.4 us (2%)
  starting transfers between devices  12.8 us (2%)
    psum x1, waiting for transfers between devices, body(): lax.psum(partial_value.astype(jnp.bfloat16), 'tensor').astype(jnp.float32)  190 us
    all_gather x1, waiting for transfers between devices, body(): lax.all_gather(routed_total, 'tensor', axis=0, tiled=True)  81.1 us
    reduce_scatter x1, waiting for transfers between devices, body(): lax.psum_scatter(terms.astype(jnp.bfloat16), 'dp', scatter_dimension=1, t...  74.4 us
    all_to_all x1, blocking collectives, body(): lax.all_to_all(filled[:, None], ('expert', 'tensor'), split_axis=0, conca...  63.7 us
    all_to_all x1, waiting for transfers between devices, body(): lax.all_to_all(summed[:, 0].astype(jnp.bfloat16), ('expert', 'tensor'), s...  49.1 us
    all_gather x1, waiting for transfers between devices, body(): everyone = lax.all_gather(arrived[:, None], 'dp', axis=1, tiled=True)  38.2 us
    all_gather x1, waiting for transfers between devices, body(): group_shared = lax.all_gather(shared_grad, 'tensor', axis=0, tiled=True)  37 us
    all_gather x1, waiting for transfers between devices, body(): lax.all_gather(grad_out, 'tensor', axis=0, tiled=True)  18.9 us
  transfers between devices with their start and end apart: 7, of which 7 were waited for; matrix products, arithmetic and copies ran while one was open for 12% of the time, Pallas kernels for 0%

commit v1 on v0

--- a/solution.py
+++ b/solution.py
@@ -140,7 +140,15 @@
     shared_total = lax.psum(partial_value.astype(jnp.bfloat16), "tensor").astype(jnp.float32)
     group_grads, group_routed = (
         lax.all_gather(grad_out, "tensor", axis=0, tiled=True),
-        lax.all_gather(routed_total, "tensor", axis=0, tiled=True),
+        jnp.concatenate(
+            lax.all_to_all(
+                jnp.stack(lax.psum(1, "tensor") * [routed_total]),
+                "tensor",
+                split_axis=0,
+                concat_axis=0,
+            ),
+            0,
+        ),
     )
     grad_group = (
         group_grads.astype(jnp.float32) + shared_total + group_routed.astype(jnp.float32)

time: 693 us -> 625 us (0.902)
  waiting for transfers between devices: 490 us -> 409 us
    all_gather x1 -> x0, waiting for transfers between devices: 81.1 us -> none  [body(): lax.all_gather(routed_total, 'tensor', axis=0, tiled=True)]
    all_gather x1, waiting for transfers between devices: 37 us -> 0.02 us  [body(): group_shared = lax.all_gather(shared_grad, 'tensor', axis=0, tiled=True)]
    reduce_scatter x1, waiting for transfers between devices: 74.4 us -> 108 us  [body(): lax.psum_scatter(terms.astype(jnp.bfloat16), 'dp', scatter_dimension=1, t...]
    psum x1, waiting for transfers between devices: 190 us -> 221 us  [body(): lax.psum(partial_value.astype(jnp.bfloat16), 'tensor').astype(jnp.float32)]
    all_gather x1, waiting for transfers between devices: 18.9 us -> 0.03 us  [body(): lax.all_gather(grad_out, 'tensor', axis=0, tiled=True)]
    all_to_all x1, waiting for transfers between devices: 49.1 us -> 40.4 us  [body(): lax.all_to_all(summed[:, 0].astype(jnp.bfloat16), ('expert', 'tensor'), s...]
  transfers between devices with their start and end apart: 7 -> 7, of which waited for: 7 -> 4; matrix products, arithmetic and copies ran while one was open for 12% -> 7% of each run, Pallas kernels for 0% -> 0%
where the time goes in v1:
time: 625 us; the launch traced here: 621 us
  waiting for transfers between devices  409 us (65%)
  local copies, waits for them, and re-layouts  73.9 us (12%)
  blocking collectives  63.7 us (10%)
  matrix products  24.1 us (4%)
  starting transfers between devices  18.6 us (3%)
  between operations  16 us (3%)
  other arithmetic  15.5 us (2%)
    psum x1, waiting for transfers between devices, body(): lax.psum(partial_value.astype(jnp.bfloat16), 'tensor').astype(jnp.float32)  221 us
    reduce_scatter x1, waiting for transfers between devices, body(): lax.psum_scatter(terms.astype(jnp.bfloat16), 'dp', scatter_dimension=1, t...  108 us
    all_to_all x1, blocking collectives, body(): lax.all_to_all(filled[:, None], ('expert', 'tensor'), split_axis=0, conca...  63.7 us
    all_to_all x1, waiting for transfers between devices, body(): lax.all_to_all(summed[:, 0].astype(jnp.bfloat16), ('expert', 'tensor'), s...  40.4 us
    all_gather x1, waiting for transfers between devices, body(): everyone = lax.all_gather(arrived[:, None], 'dp', axis=1, tiled=True)  39.2 us
    all_to_all x1, starting transfers between devices, body(): lax.all_to_all(summed[:, 0].astype(jnp.bfloat16), ('expert', 'tensor'), s...  12.7 us
  transfers between devices with their start and end apart: 7, of which 4 were waited for; matrix products, arithmetic and copies ran while one was open for 7% of the time, Pallas kernels for 0%

profile of v1, /device:TPU:1, one launch (start us, length us, event | category | flops | bytes accessed | tf_op | source)
XLA Modules:
  0.0 621.2 jit_solution(18179647012433842865)
XLA Ops:
  13.5 2.1 mul.107
  15.6 2.5 mul.108
  20.0 3.0 gather_fusion
  23.1 2.4 broadcast_in_dim_reshape.4
  25.4 63.7 %all_to_all.23 = bf16[64,1,5,2048]{3,2,1,0:T(8,128)(2,1)S(1)} all-to-all(bf16[64,1,5,2048]{3,2,1,0:T(8,128)(2,1)S(1)} %bitcast.50), channel_id=1, replica_groups=mesh['dp'=4,'expert'=8,'tensor'=8] {'expert','tensor'}, dimensions={0} | all-to-all | bytes 2621440 | tf_op jit(solution)/shard_map/all_to_all | solution.py:97
  89.1 2.0 copy.36
  91.1 2.3 copy.40
  93.4 3.6 reshape.164
  98.9 3.5 copy.38
  102.3 3.9 reshape.163
  106.2 2.8 copy.39
  109.0 39.2 %all-gather.9.cloned.1.call-done = bf16[256,1,5,2048]{3,0,2,1:T(8,128)(2,1)} async-done(((bf16[64,1,5,2048]{3,0,2,1:T(8,128)(2,1)}), bf16[256,1,5,2048]{3,0,2,1:T(8,128)(2,1)}) %all-gather.9.cloned.1.call-update) | async-done | bytes 5242896 | tf_op jit(solution)/shard_map/all_gather | solution.py:100
  148.2 8.9 %copy.37 = bf16[256,1,5,2048]{3,2,0,1:T(8,128)(2,1)} copy(bf16[256,1,5,2048]{3,0,2,1:T(8,128)(2,1)} %all-gather.9.cloned.1.call-done) | data formatting | bytes 10485760 | tf_op jit(solution)/shard_map/all_gather | solution.py:100
  157.1 10.0 %reshape.157 = bf16[1280,2048]{1,0:T(8,128)(2,1)} reshape(bf16[256,1,5,2048]{3,2,0,1:T(8,128)(2,1)} %copy.37) | data formatting | bytes 10485760 | tf_op jit(solution)/shard_map/reshape.6
  167.2 5.1 fusion.5
  172.3 3.3 fusion.3
  175.6 5.0 fusion.1
  180.6 9.8 %convert_element_type.150 = bf16[1,4,64,5,2048]{4,3,2,1,0:T(8,128)(2,1)} reshape(bf16[1,1280,2048]{2,1,0:T(8,128)(2,1)} %fusion.1) | data formatting | bytes 10485760 | tf_op jit(solution)/shard_map/convert_element_type | solution.py:113
  193.0 108.0 %reduce-scatter.2.cloned.1.call-done = bf16[1,1,64,5,2048]{4,3,2,1,0:T(8,128)(2,1)} async-done(((bf16[1,4,64,5,2048]{4,3,2,1,0:T(8,128)(2,1)}), bf16[1,1,64,5,2048]{4,3,2,1,0:T(8,128)(2,1)}) %reduce-scatter.2.cloned.1.call-update) | async-done | bytes 1310736 | tf_op jit(solution)/shard_map/reduce_scatter | solution.py:112
  301.1 12.7 %all-to-all-start.1 = ((bf16[1,64,5,2048]{3,2,0,1:T(8,128)(2,1)}), bf16[1,64,5,2048]{3,2,0,1:T(8,128)(2,1)}, u32[]{:S(2)}, u32[]{:S(2)}) async-start(bf16[1,64,5,2048]{3,2,0,1:T(8,128)(2,1)} %bitcast.51), calls=%async_computation.2 | async-start | bytes 4194304 | tf_op jit(solution)/shard_map/all_to_all | solution.py:115
  313.9 3.8 fusion.33
  319.2 3.3 add_convert_fusion.1
  322.5 40.4 %all-to-all-done.1 = bf16[1,64,5,2048]{3,2,0,1:T(8,128)(2,1)} async-done(((bf16[1,64,5,2048]{3,2,0,1:T(8,128)(2,1)}), bf16[1,64,5,2048]{3,2,0,1:T(8,128)(2,1)}, u32[]{:S(2)}, u32[]{:S(2)}) %all-to-all-start.1) | async-done | bytes 1310752 | tf_op jit(solution)/shard_map/all_to_all | solution.py:115
  362.9 2.5 reshape.165
  365.4 2.7 gather_fusion.1
  368.1 2.5 reshape.161
  370.6 3.0 reduce_sum.32
  373.6 2.5 stack.2
  376.1 5.7 all-to-all-start.2
  381.9 221.2 %all-reduce.3.cloned.1.call-done = bf16[1024,2048]{1,0:T(8,128)(2,1)} async-done(((bf16[1024,2048]{1,0:T(8,128)(2,1)}), bf16[1024,2048]{1,0:T(8,128)(2,1)}) %all-reduce.3.cloned.1.call-update) | async-done | bytes 4194320 | tf_op jit(solution)/shard_map/psum | solution.py:140
  603.1 7.6 %fusion = bf16[1024,2048]{1,0:T(8,128)(2,1)S(1)} fusion(bf16[1024,2048]{1,0:T(8,128)(2,1)} %all-reduce.3.cloned.1.call-done, bf16[1024,2048]{1,0:T(8,128)(2,1)} %all-gather.5.cloned.1.call-done, bf16[8,128,2048]{2,1,0:T(8,128)(2,1)} %all-to-all-done.2), kind=kLoop, calls=%fused_computation.5 | loop fusion | flops 12582912 | bytes 16777216 | tf_op jit(solution)/shard_map/convert_element_type | solution.py:155
  611.6 2.1 convolution_convert_fusion
  (65 shorter events, 14.3 us)
Async XLA Ops:
  8.0 164.3 %copy-start = (bf16[1,2048,352]{1,2,0:T(8,128)(2,1)S(1)}, bf16[1,2048,352]{1,2,0:T(8,128)(2,1)}, u32[]{:S(2)}) copy-start(bf16[1,2048,352]{1,2,0:T(8,128)(2,1)} %param.21) | copy-start | bytes 4325380
  8.0 140.2 %all-gather.9.cloned.1.call-start = ((), (), s32[]{:S(2)}) async-start(), calls=%async_computation.8 | async-start | bytes 6553600 | tf_op jit(solution)/shard_map/all_gather | solution.py:100
  89.1 2.0 copy-start.6
  91.1 210.0 %reduce-scatter.2.cloned.1.call-start = ((), (), s32[]{:S(2)}) async-start(), calls=%async_computation.7 | async-start | bytes 10485760 | tf_op jit(solution)/shard_map/reduce_scatter | solution.py:112
  167.2 5.1 copy-start.2
  172.3 3.3 copy-start.5
  190.4 1.0 copy-start.3
  190.4 123.4 %all-gather.7.cloned.1.call-start = ((), (), s32[]{:S(2)}) async-start(), calls=%async_computation.5 | async-start | bytes 4718592 | tf_op jit(solution)/shard_map/all_gather | solution.py:126
  192.4 189.4 %all-gather.5.cloned.1.call-start = ((), (), s32[]{:S(2)}) async-start(), calls=%async_computation.4 | async-start | bytes 4718592 | tf_op jit(solution)/shard_map/all_gather | solution.py:142
  301.1 12.8 %copy-start.11 = (bf16[176,2048]{1,0:T(8,128)(2,1)S(1)}, bf16[176,2048]{1,0:T(8,128)(2,1)}, u32[]{:S(2)}) copy-start(bf16[176,2048]{1,0:T(8,128)(2,1)} %param.28) | copy-start | bytes 2162692
  301.1 61.8 %all-to-all-start.1 = ((bf16[1,64,5,2048]{3,2,0,1:T(8,128)(2,1)}), bf16[1,64,5,2048]{3,2,0,1:T(8,128)(2,1)}, u32[]{:S(2)}, u32[]{:S(2)}) async-start(bf16[1,64,5,2048]{3,2,0,1:T(8,128)(2,1)} %bitcast.51), calls=%async_computation.2 | async-start | bytes 4194304 | tf_op jit(solution)/shard_map/all_to_all | solution.py:115
  313.8 4.0 copy-start.4
  313.8 3.9 copy-start.8
  313.8 3.9 copy-start.9
  313.8 289.3 %all-reduce.3.cloned.1.call-start = ((), (), s32[]{:S(2)}) async-start(), calls=%async_computation.6 | async-start | bytes 8388608 | tf_op jit(solution)/shard_map/psum | solution.py:140
  317.7 1.4 copy-start.7
  376.1 227.0 %all-to-all-start.2 = ((bf16[8,128,2048]{2,1,0:T(8,128)(2,1)}), bf16[8,128,2048]{2,1,0:T(8,128)(2,1)}, u32[]{:S(2)}, u32[]{:S(2)}) async-start(bf16[8,128,2048]{2,1,0:T(8,128)(2,1)} %stack.2), calls=%async_computation.3 | async-start | bytes 8388608 | tf_op jit(solution)/shard_map/all_to_all | solution.py:144
  381.8 229.7 %copy-start.10 = (bf16[256,2048]{1,0:T(8,128)(2,1)S(1)}, bf16[256,2048]{1,0:T(8,128)(2,1)}, u32[]{:S(2)}) copy-start(bf16[256,2048]{1,0:T(8,128)(2,1)} %param.29) | copy-start | bytes 3145732
  611.6 2.1 copy-start.1
Sparse Core Ops, SparseCore 0:
  91.2 57.0 all-gather.8
  190.6 110.4 reduce-scatter.1
Sparse Core Ops, SparseCore 1:
  194.1 92.3 all-gather.6
  289.0 90.4 all-gather.4
  381.9 221.1 all-reduce.2
